TPU v7x, 1024 devices: a whole 4x4x32 slice. The times are simulated.
1024 devices in a mesh: fifth: 16 (over y, z_hi), space: 64 (over z_lo, x, core).
Axes of the slice: x: 4, y: 4, z: 32 (z_hi: 4, z_lo: 8; z = z_hi * 8 + z_lo), core: 2. Of those that a mesh axis runs over, the one named last changes fastest.
Arguments:
- spinor: float32 [32, 24, 64, 512], P('fifth', None, 'space'), may hold values from -6 to 6
- gauge_links: float32 [4, 18, 64, 512], P(None, None, 'space'), may hold values from -1 to 1, as said below
Outputs:
- filtered: float32 [32, 24, 64, 512], P('fifth', None, 'space')
Inputs may be any that keep to these rules, and one draw needn't show every extreme that they name: `gauge_links`: every link is a special unitary 3 x 3 complex matrix.
All inputs are finite; a program needn't handle non-finite values.
Results may differ from a plain program's by a relative error of at most 0.00002.
Values sent between devices are 32-bit elements; how exact they have to be, the bound alone decides.
A program may use at most 32 MiB of HBM per device.

v0:
```python
import jax
import jax.numpy as jnp
from jax import lax
from jax.sharding import PartitionSpec as P

L = 8
DEGREE = 4


wall_height = 1.8
quark_mass = 0.1
filter_center = 0.5
filter_radius = 8.0
gamma_block = (((1, 1), (0, 1)), ((1, 2), (0, 0)), ((0, 1), (1, 3)), ((0, 0), (1, 0)))
gamma_adjoint = (((1, 3), (0, 3)), ((1, 0), (0, 2)), ((0, 3), (1, 1)), ((0, 0), (1, 0)))


def shifted(value, axis, steps):
    count = lax.axis_size(axis)
    pairs = [(source, (source + steps) % count) for source in range(count)]
    return lax.ppermute(value, axis, pairs)


def padded_2(block, sides, width):
    for axis, dim in sides:
        count = lax.axis_size(axis)
        forward = [(i, i + 1) for i in range(count - 1)]
        forward.append((count - 1, 0))
        backward = [(target, source) for source, target in forward]
        low = lax.ppermute(
            lax.slice_in_dim(block, block.shape[dim] - width, None, axis=dim), axis, forward
        )
        high = lax.ppermute(lax.slice_in_dim(block, 0, width, axis=dim), axis, backward)
        block = jnp.concatenate([low, block, high], axis=dim)
    return block


def swapped(value, axis, distance):
    mask = 2**distance
    pairs = [(source, source ^ mask) for source in range(lax.axis_size(axis))]
    return lax.ppermute(value, axis, pairs)


def times_unit(values, quarter):
    for repeat in range(quarter % 4):
        values = jnp.stack([-values[..., 1, :, :], values[..., 0, :, :]], axis=-3)
    return values


def project(current, direction, parity):
    halves_list = []
    for top_row in range(2):
        source, quarter = gamma_block[direction][top_row]
        blended = times_unit(current[..., 2 + source, :, :, :, :], quarter)
        halves_list.append(current[..., top_row, :, :, :, :] + parity * blended)
    return jnp.stack(halves_list, axis=-5)


def rebuild(half_spinor, direction, parity):
    lower_part = []
    for row_index in range(2):
        source, quarter = gamma_adjoint[direction][row_index]
        lower_part.append(parity * times_unit(half_spinor[..., source, :, :, :, :], quarter))
    return jnp.concatenate([half_spinor, jnp.stack(lower_part, axis=-5)], axis=-5)


def colour_mul(link_matrix, half_spinor, dagger):
    link_re = link_matrix[:, :, 0]
    link_im = link_matrix[:, :, 1]
    if dagger:
        link_re = jnp.swapaxes(link_re, 0, 1)
        link_im = -jnp.swapaxes(link_im, 0, 1)
    result_re = None
    result_im = None
    for column in range(3):
        half_re = half_spinor[..., column : column + 1, 0, :, :]
        half_im = half_spinor[..., column : column + 1, 1, :, :]
        term_re = link_re[:, column] * half_re - link_im[:, column] * half_im
        term_im = link_re[:, column] * half_im + link_im[:, column] * half_re
        if result_re is None:
            result_re, result_im = (term_re, term_im)
        else:
            result_re = result_re + term_re
            result_im = result_im + term_im
    return jnp.stack([result_re, result_im], axis=-3)


def space_shift(values, stride, extent, forward):
    position = jnp.arange(values.shape[-1]) // stride % extent
    if forward:
        inside_roll = jnp.roll(values, -stride, axis=-1)
        outside_roll = jnp.roll(values, (extent - 1) * stride, axis=-1)
        return jnp.where(position == extent - 1, outside_roll, inside_roll)
    inside_roll = jnp.roll(values, stride, axis=-1)
    outside_roll = jnp.roll(values, -(extent - 1) * stride, axis=-1)
    return jnp.where(position == 0, outside_roll, inside_roll)


def space_hops(current, gauge, extent):
    summed = jnp.zeros_like(current)
    for direction in range(3):
        stride = extent**direction
        forward_half = space_shift(project(current, direction, -1.0), stride, extent, True)
        summed = summed + rebuild(
            colour_mul(gauge[direction], forward_half, False), direction, -1.0
        )
        behind = colour_mul(gauge[direction], project(current, direction, 1.0), True)
        summed = summed + rebuild(space_shift(behind, stride, extent, False), direction, 1.0)
    return summed


def chiral_sign(current):
    return jnp.concatenate([current[:, 0:2], -current[:, 2:4]], axis=1)


def on_device(spinor, gauge_links):
    slices = spinor.shape[0]
    time_depth = spinor.shape[2]
    sites = spinor.shape[3]
    start_field = spinor.reshape(slices, 4, 3, 2, time_depth, sites)
    gauge = gauge_links.reshape(4, 3, 3, 2, time_depth, sites)
    time_links = gauge[3]
    space_count = lax.axis_size("space")
    space_place = lax.axis_index("space")
    fifth_count = lax.axis_size("fifth")
    fifth_place = lax.axis_index("fifth")
    low_sign = jnp.where(space_place == 0, -1.0, 1.0)
    high_sign = jnp.where(space_place == space_count - 1, -1.0, 1.0)
    low_mass = jnp.where(fifth_place == 0, -quark_mass, 1.0)
    high_mass = jnp.where(fifth_place == fifth_count - 1, -quark_mass, 1.0)
    link_below = shifted(time_links, "space", 1)
    links_behind = jnp.concatenate([link_below, time_links[..., : time_depth - 1, :]], axis=-2)

    def dirac(current):
        hop_sum = space_hops(current, gauge, L)
        padded = padded_2(current, (("space", 4),), 1)
        extended = jnp.concatenate(
            [padded[..., 0:1, :] * low_sign, current, padded[..., time_depth + 1 :, :] * high_sign],
            axis=-2,
        )
        forward_half = project(extended[..., 2:, :], 3, -1.0)
        behind = colour_mul(links_behind, project(extended[..., :time_depth, :], 3, 1.0), True)
        hop_sum = hop_sum + rebuild(colour_mul(time_links, forward_half, False), 3, -1.0)
        hop_sum = hop_sum + rebuild(behind, 3, 1.0)
        lower_chiral = shifted(current[slices - 1 :, 0:2], "fifth", 1) * low_mass
        upper_chiral = shifted(current[0:1, 2:4], "fifth", -1) * high_mass
        down_half = jnp.concatenate([lower_chiral, current[: slices - 1, 0:2]], axis=0)
        up_half = jnp.concatenate([current[1:, 2:4], upper_chiral], axis=0)
        chiral_hop = jnp.concatenate([down_half, up_half], axis=1)
        return (5.0 - wall_height) * current - 0.5 * hop_sum - chiral_hop

    def mirror(current):
        bit_count = lax.axis_size("fifth").bit_length() - 1
        for bit_index in range(bit_count):
            current = swapped(current, "fifth", bit_index)
        return jnp.flip(current, axis=0)

    def apply_hermitian(current):
        return mirror(chiral_sign(dirac(current)))

    previous = start_field
    current = (apply_hermitian(previous) - filter_center * previous) / filter_radius
    for order in range(1, DEGREE):
        following = (
            2.0 * (apply_hermitian(current) - filter_center * current) / filter_radius - previous
        )
        previous, current = (current, following)
    return current.reshape(slices, 24, time_depth, sites)


def solution(mesh):
    placed = (P("fifth", None, "space", None), P(None, None, "space", None))
    return jax.shard_map(
        on_device,
        mesh=mesh,
        in_specs=placed,
        out_specs=P("fifth", None, "space", None),
        check_vma=False,
    )
```

profile of v0, /device:TPU:8, one launch (start us, length us, event | category | flops | bytes accessed | tf_op | source)
XLA Modules:
  0.0 443.4 jit_solution(11713752353498378928)
XLA Ops:
  1.0 14.8 %collective-permute-start = (f32[2,4,3,2,1,512]{5,3,2,0,4,1:T(2,128)S(1)}, f32[2,4,3,2,1,512]{5,3,2,0,4,1:T(2,128)S(1)}, u32[]{:S(2)}, u32[]{:S(2)}) collective-permute-start(f32[2,4,3,2,1,512]{5,3,2,0,4,1:T(2,128)S(1)} %copy.1268), channel_id=1, source_target_pairs={{1,0},{2,1},{3,2},{4,3},{5,4},{6,5},{7,6},{8,7},{9,8},{10,9},{11,1... | collective-permute-start | bytes 294920 | tf_op jit(solution)/shard_map/ppermute | solution.py:33
  19.8 15.4 %collective-permute-start.4 = (f32[1,2,3,2,1,512]{5,3,2,0,4,1:T(2,128)S(1)}, f32[1,2,3,2,1,512]{5,3,2,0,4,1:T(2,128)S(1)}, u32[]{:S(2)}, u32[]{:S(2)}) collective-permute-start(f32[1,2,3,2,1,512]{5,3,2,0,4,1:T(2,128)S(1)} %get-tuple-element.161), channel_id=1, source_target_pairs={{0,960},{64,0},{128,64},{192,128},{256,192},{320,256},{384,320},{4... | collective-permute-start | bytes 73736 | tf_op jit(solution)/shard_map/ppermute | solution.py:21
  44.3 6.4 %collective-permute-done.3 = f32[1,2,3,2,1,512]{5,3,2,0,4,1:T(2,128)S(1)} collective-permute-done((f32[1,2,3,2,1,512]{5,3,2,0,4,1:T(2,128)S(1)}, f32[1,2,3,2,1,512]{5,3,2,0,4,1:T(2,128)S(1)}, u32[]{:S(2)}, u32[]{:S(2)}) %collective-permute-start.3) | collective-permute-done | bytes 24608 | tf_op jit(solution)/shard_map/ppermute | solution.py:21
  58.5 18.9 %collective-permute-done.5 = f32[2,4,3,2,1,512]{5,3,2,0,4,1:T(2,128)S(1)} collective-permute-done((f32[2,4,3,2,1,512]{5,3,2,0,4,1:T(2,128)S(1)}, f32[2,4,3,2,1,512]{5,3,2,0,4,1:T(2,128)S(1)}, u32[]{:S(2)}, u32[]{:S(2)}) %collective-permute-start.5) | collective-permute-done | bytes 98336 | tf_op jit(solution)/shard_map/ppermute | solution.py:41
  77.4 13.1 %collective-permute-start.6 = (f32[2,4,3,2,1,512]{5,3,2,0,4,1:T(2,128)S(1)}, f32[2,4,3,2,1,512]{5,3,2,0,4,1:T(2,128)S(1)}, u32[]{:S(2)}, u32[]{:S(2)}) collective-permute-start(f32[2,4,3,2,1,512]{5,3,2,0,4,1:T(2,128)S(1)} %collective-permute-done.5), channel_id=1, source_target_pairs={{0,128},{64,192},{128,0},{192,64},{256,384},{320,448},{384,256},{4... | collective-permute-start | bytes 294920 | tf_op jit(solution)/shard_map/ppermute | solution.py:41
  90.4 19.5 %collective-permute-done.6 = f32[2,4,3,2,1,512]{5,3,2,0,4,1:T(2,128)S(1)} collective-permute-done((f32[2,4,3,2,1,512]{5,3,2,0,4,1:T(2,128)S(1)}, f32[2,4,3,2,1,512]{5,3,2,0,4,1:T(2,128)S(1)}, u32[]{:S(2)}, u32[]{:S(2)}) %collective-permute-start.6) | collective-permute-done | bytes 98336 | tf_op jit(solution)/shard_map/ppermute | solution.py:41
  131.3 12.5 %collective-permute-start.9 = (f32[2,4,3,2,1,512]{5,3,2,0,4,1:T(2,128)S(1)}, f32[2,4,3,2,1,512]{5,3,2,0,4,1:T(2,128)S(1)}, u32[]{:S(2)}, u32[]{:S(2)}) collective-permute-start(f32[2,4,3,2,1,512]{5,3,2,0,4,1:T(2,128)S(1)} %get-tuple-element.6), channel_id=1, source_target_pairs={{1,0},{2,1},{3,2},{4,3},{5,4},{6,5},{7,6},{8,7},{9,8},{10,9},{11,1... | collective-permute-start | bytes 294920 | tf_op jit(solution)/shard_map/ppermute | solution.py:33
  150.0 9.7 %collective-permute-start.11 = (f32[1,2,3,2,1,512]{5,3,2,0,4,1:T(2,128)S(1)}, f32[1,2,3,2,1,512]{5,3,2,0,4,1:T(2,128)S(1)}, u32[]{:S(2)}, u32[]{:S(2)}) collective-permute-start(f32[1,2,3,2,1,512]{5,3,2,0,4,1:T(2,128)S(1)} %get-tuple-element.133), channel_id=1, source_target_pairs={{0,64},{64,128},{128,192},{192,256},{256,320},{320,384},{384,448},... | collective-permute-start | bytes 73736 | tf_op jit(solution)/shard_map/ppermute | solution.py:21
  160.7 6.6 %collective-permute-done.11 = f32[1,2,3,2,1,512]{5,3,2,0,4,1:T(2,128)S(1)} collective-permute-done((f32[1,2,3,2,1,512]{5,3,2,0,4,1:T(2,128)S(1)}, f32[1,2,3,2,1,512]{5,3,2,0,4,1:T(2,128)S(1)}, u32[]{:S(2)}, u32[]{:S(2)}) %collective-permute-start.11) | collective-permute-done | bytes 24608 | tf_op jit(solution)/shard_map/ppermute | solution.py:21
  168.6 7.1 %collective-permute-start.13 = (f32[2,4,3,2,1,512]{5,1,4,3,2,0:T(4,128)S(1)}, f32[2,4,3,2,1,512]{5,1,4,3,2,0:T(4,128)S(1)}, u32[]{:S(2)}, u32[]{:S(2)}) collective-permute-start(f32[2,4,3,2,1,512]{5,1,4,3,2,0:T(4,128)S(1)} %pad_maximum_fusion.1), channel_id=1, source_target_pairs={{0,64},{64,0},{128,192},{192,128},{256,320},{320,256},{384,448},{4... | collective-permute-start | bytes 294920 | tf_op jit(solution)/shard_map/ppermute | solution.py:41
  175.8 13.5 %collective-permute-done.13 = f32[2,4,3,2,1,512]{5,1,4,3,2,0:T(4,128)S(1)} collective-permute-done((f32[2,4,3,2,1,512]{5,1,4,3,2,0:T(4,128)S(1)}, f32[2,4,3,2,1,512]{5,1,4,3,2,0:T(4,128)S(1)}, u32[]{:S(2)}, u32[]{:S(2)}) %collective-permute-start.13) | collective-permute-done | bytes 98336 | tf_op jit(solution)/shard_map/ppermute | solution.py:41
  191.9 22.1 %collective-permute-done.14 = f32[2,4,3,2,1,512]{5,1,4,3,2,0:T(4,128)S(1)} collective-permute-done((f32[2,4,3,2,1,512]{5,1,4,3,2,0:T(4,128)S(1)}, f32[2,4,3,2,1,512]{5,1,4,3,2,0:T(4,128)S(1)}, u32[]{:S(2)}, u32[]{:S(2)}) %collective-permute-start.14) | collective-permute-done | bytes 98336 | tf_op jit(solution)/shard_map/ppermute | solution.py:41
  234.2 12.4 %collective-permute-start.17 = (f32[2,4,3,2,1,512]{5,3,2,0,4,1:T(2,128)S(1)}, f32[2,4,3,2,1,512]{5,3,2,0,4,1:T(2,128)S(1)}, u32[]{:S(2)}, u32[]{:S(2)}) collective-permute-start(f32[2,4,3,2,1,512]{5,3,2,0,4,1:T(2,128)S(1)} %copy.1596), channel_id=1, source_target_pairs={{1,0},{2,1},{3,2},{4,3},{5,4},{6,5},{7,6},{8,7},{9,8},{10,9},{11,1... | collective-permute-start | bytes 294920 | tf_op jit(solution)/shard_map/ppermute | solution.py:33
  252.1 12.6 %collective-permute-start.20 = (f32[1,2,3,2,1,512]{5,1,4,3,2,0:T(2,128)S(1)}, f32[1,2,3,2,1,512]{5,1,4,3,2,0:T(2,128)S(1)}, u32[]{:S(2)}, u32[]{:S(2)}) collective-permute-start(f32[1,2,3,2,1,512]{5,1,4,3,2,0:T(2,128)S(1)} %get-tuple-element.109), channel_id=1, source_target_pairs={{0,960},{64,0},{128,64},{192,128},{256,192},{320,256},{384,320},{4... | collective-permute-start | bytes 73736 | tf_op jit(solution)/shard_map/ppermute | solution.py:21
  267.8 7.6 %collective-permute-start.21 = (f32[2,4,3,2,1,512]{5,1,4,3,2,0:T(4,128)S(1)}, f32[2,4,3,2,1,512]{5,1,4,3,2,0:T(4,128)S(1)}, u32[]{:S(2)}, u32[]{:S(2)}) collective-permute-start(f32[2,4,3,2,1,512]{5,1,4,3,2,0:T(4,128)S(1)} %pad_maximum_fusion.2), channel_id=1, source_target_pairs={{0,64},{64,0},{128,192},{192,128},{256,320},{320,256},{384,448},{4... | collective-permute-start | bytes 294920 | tf_op jit(solution)/shard_map/ppermute | solution.py:41
  275.4 7.6 %collective-permute-done.21 = f32[2,4,3,2,1,512]{5,1,4,3,2,0:T(4,128)S(1)} collective-permute-done((f32[2,4,3,2,1,512]{5,1,4,3,2,0:T(4,128)S(1)}, f32[2,4,3,2,1,512]{5,1,4,3,2,0:T(4,128)S(1)}, u32[]{:S(2)}, u32[]{:S(2)}) %collective-permute-start.21) | collective-permute-done | bytes 98336 | tf_op jit(solution)/shard_map/ppermute | solution.py:41
  283.1 14.9 %collective-permute-start.22 = (f32[2,4,3,2,1,512]{5,1,4,3,2,0:T(4,128)S(1)}, f32[2,4,3,2,1,512]{5,1,4,3,2,0:T(4,128)S(1)}, u32[]{:S(2)}, u32[]{:S(2)}) collective-permute-start(f32[2,4,3,2,1,512]{5,1,4,3,2,0:T(4,128)S(1)} %collective-permute-done.21), channel_id=1, source_target_pairs={{0,128},{64,192},{128,0},{192,64},{256,384},{320,448},{384,256},{4... | collective-permute-start | bytes 294920 | tf_op jit(solution)/shard_map/ppermute | solution.py:41
  298.0 11.2 %collective-permute-done.22 = f32[2,4,3,2,1,512]{5,1,4,3,2,0:T(4,128)S(1)} collective-permute-done((f32[2,4,3,2,1,512]{5,1,4,3,2,0:T(4,128)S(1)}, f32[2,4,3,2,1,512]{5,1,4,3,2,0:T(4,128)S(1)}, u32[]{:S(2)}, u32[]{:S(2)}) %collective-permute-start.22) | collective-permute-done | bytes 98336 | tf_op jit(solution)/shard_map/ppermute | solution.py:41
  316.0 23.3 %collective-permute-start.24 = (f32[2,4,3,2,1,512]{5,1,4,3,2,0:T(4,128)S(1)}, f32[2,4,3,2,1,512]{5,1,4,3,2,0:T(4,128)S(1)}, u32[]{:S(2)}, u32[]{:S(2)}) collective-permute-start(f32[2,4,3,2,1,512]{5,1,4,3,2,0:T(4,128)S(1)} %collective-permute-done.23), channel_id=1, source_target_pairs={{0,512},{64,576},{128,640},{192,704},{256,768},{320,832},{384,896}... | collective-permute-start | bytes 294920 | tf_op jit(solution)/shard_map/ppermute | solution.py:41
  346.7 12.4 %collective-permute-start.25 = (f32[2,4,3,2,1,512]{5,3,2,0,4,1:T(2,128)S(1)}, f32[2,4,3,2,1,512]{5,3,2,0,4,1:T(2,128)S(1)}, u32[]{:S(2)}, u32[]{:S(2)}) collective-permute-start(f32[2,4,3,2,1,512]{5,3,2,0,4,1:T(2,128)S(1)} %copy.1752), channel_id=1, source_target_pairs={{1,0},{2,1},{3,2},{4,3},{5,4},{6,5},{7,6},{8,7},{9,8},{10,9},{11,1... | collective-permute-start | bytes 294920 | tf_op jit(solution)/shard_map/ppermute | solution.py:33
  363.7 13.5 %collective-permute-start.28 = (f32[1,2,3,2,1,512]{5,1,4,3,2,0:T(2,128)S(1)}, f32[1,2,3,2,1,512]{5,1,4,3,2,0:T(2,128)S(1)}, u32[]{:S(2)}, u32[]{:S(2)}) collective-permute-start(f32[1,2,3,2,1,512]{5,1,4,3,2,0:T(2,128)S(1)} %get-tuple-element.86), channel_id=1, source_target_pairs={{0,960},{64,0},{128,64},{192,128},{256,192},{320,256},{384,320},{4... | collective-permute-start | bytes 73736 | tf_op jit(solution)/shard_map/ppermute | solution.py:21
  386.6 16.6 %collective-permute-done.29 = f32[2,4,3,2,1,512]{5,1,4,3,2,0:T(4,128)S(1)} collective-permute-done((f32[2,4,3,2,1,512]{5,1,4,3,2,0:T(4,128)S(1)}, f32[2,4,3,2,1,512]{5,1,4,3,2,0:T(4,128)S(1)}, u32[]{:S(2)}, u32[]{:S(2)}) %collective-permute-start.29) | collective-permute-done | bytes 98336 | tf_op jit(solution)/shard_map/ppermute | solution.py:41
  403.2 6.3 %collective-permute-start.30 = (f32[2,4,3,2,1,512]{5,1,4,3,2,0:T(4,128)S(1)}, f32[2,4,3,2,1,512]{5,1,4,3,2,0:T(4,128)S(1)}, u32[]{:S(2)}, u32[]{:S(2)}) collective-permute-start(f32[2,4,3,2,1,512]{5,1,4,3,2,0:T(4,128)S(1)} %collective-permute-done.29), channel_id=1, source_target_pairs={{0,128},{64,192},{128,0},{192,64},{256,384},{320,448},{384,256},{4... | collective-permute-start | bytes 294920 | tf_op jit(solution)/shard_map/ppermute | solution.py:41
  409.6 18.5 %collective-permute-done.30 = f32[2,4,3,2,1,512]{5,1,4,3,2,0:T(4,128)S(1)} collective-permute-done((f32[2,4,3,2,1,512]{5,1,4,3,2,0:T(4,128)S(1)}, f32[2,4,3,2,1,512]{5,1,4,3,2,0:T(4,128)S(1)}, u32[]{:S(2)}, u32[]{:S(2)}) %collective-permute-start.30) | collective-permute-done | bytes 98336 | tf_op jit(solution)/shard_map/ppermute | solution.py:41
  (689 shorter events, 122.0 us)
Async XLA Ops:
  1.0 49.8 %collective-permute-start = (f32[2,4,3,2,1,512]{5,3,2,0,4,1:T(2,128)S(1)}, f32[2,4,3,2,1,512]{5,3,2,0,4,1:T(2,128)S(1)}, u32[]{:S(2)}, u32[]{:S(2)}) collective-permute-start(f32[2,4,3,2,1,512]{5,3,2,0,4,1:T(2,128)S(1)} %copy.1268), channel_id=1, source_target_pairs={{1,0},{2,1},{3,2},{4,3},{5,4},{6,5},{7,6},{8,7},{9,8},{10,9},{11,1... | collective-permute-start | bytes 294920 | tf_op jit(solution)/shard_map/ppermute | solution.py:33
  15.8 35.2 %collective-permute-start.2 = (f32[2,4,3,2,1,512]{5,3,2,0,4,1:T(2,128)S(1)}, f32[2,4,3,2,1,512]{5,3,2,0,4,1:T(2,128)S(1)}, u32[]{:S(2)}, u32[]{:S(2)}) collective-permute-start(f32[2,4,3,2,1,512]{5,3,2,0,4,1:T(2,128)S(1)} %copy.1268), channel_id=1, source_target_pairs={{0,1},{1,2},{2,3},{3,4},{4,5},{5,6},{6,7},{7,8},{8,9},{9,10},{10,1... | collective-permute-start | bytes 294920 | tf_op jit(solution)/shard_map/ppermute | solution.py:30
  17.8 33.0 %collective-permute-start.1 = (f32[3,3,2,1,512]{4,1,0,3,2:T(4,128)S(1)}, f32[3,3,2,1,512]{4,1,0,3,2:T(4,128)S(1)}, u32[]{:S(2)}, u32[]{:S(2)}) collective-permute-start(f32[3,3,2,1,512]{4,1,0,3,2:T(4,128)S(1)} %copy.1413), channel_id=1, source_target_pairs={{0,1},{1,2},{2,3},{3,4},{4,5},{5,6},{6,7},{7,8},{8,9},{9,10},{10,1... | collective-permute-start | bytes 110600 | tf_op jit(solution)/shard_map/ppermute | solution.py:21
  19.8 24.5 %collective-permute-start.4 = (f32[1,2,3,2,1,512]{5,3,2,0,4,1:T(2,128)S(1)}, f32[1,2,3,2,1,512]{5,3,2,0,4,1:T(2,128)S(1)}, u32[]{:S(2)}, u32[]{:S(2)}) collective-permute-start(f32[1,2,3,2,1,512]{5,3,2,0,4,1:T(2,128)S(1)} %get-tuple-element.161), channel_id=1, source_target_pairs={{0,960},{64,0},{128,64},{192,128},{256,192},{320,256},{384,320},{4... | collective-permute-start | bytes 73736 | tf_op jit(solution)/shard_map/ppermute | solution.py:21
  35.2 15.6 %collective-permute-start.3 = (f32[1,2,3,2,1,512]{5,3,2,0,4,1:T(2,128)S(1)}, f32[1,2,3,2,1,512]{5,3,2,0,4,1:T(2,128)S(1)}, u32[]{:S(2)}, u32[]{:S(2)}) collective-permute-start(f32[1,2,3,2,1,512]{5,3,2,0,4,1:T(2,128)S(1)} %get-tuple-element.160), channel_id=1, source_target_pairs={{0,64},{64,128},{128,192},{192,256},{256,320},{320,384},{384,448},... | collective-permute-start | bytes 73736 | tf_op jit(solution)/shard_map/ppermute | solution.py:21
  52.3 25.1 %collective-permute-start.5 = (f32[2,4,3,2,1,512]{5,3,2,0,4,1:T(2,128)S(1)}, f32[2,4,3,2,1,512]{5,3,2,0,4,1:T(2,128)S(1)}, u32[]{:S(2)}, u32[]{:S(2)}) collective-permute-start(f32[2,4,3,2,1,512]{5,3,2,0,4,1:T(2,128)S(1)} %pad_maximum_fusion), channel_id=1, source_target_pairs={{0,64},{64,0},{128,192},{192,128},{256,320},{320,256},{384,448},{4... | collective-permute-start | bytes 294920 | tf_op jit(solution)/shard_map/ppermute | solution.py:41
  77.4 32.6 %collective-permute-start.6 = (f32[2,4,3,2,1,512]{5,3,2,0,4,1:T(2,128)S(1)}, f32[2,4,3,2,1,512]{5,3,2,0,4,1:T(2,128)S(1)}, u32[]{:S(2)}, u32[]{:S(2)}) collective-permute-start(f32[2,4,3,2,1,512]{5,3,2,0,4,1:T(2,128)S(1)} %collective-permute-done.5), channel_id=1, source_target_pairs={{0,128},{64,192},{128,0},{192,64},{256,384},{320,448},{384,256},{4... | collective-permute-start | bytes 294920 | tf_op jit(solution)/shard_map/ppermute | solution.py:41
  129.4 38.2 %collective-permute-start.10 = (f32[2,4,3,2,1,512]{5,3,2,0,4,1:T(2,128)S(1)}, f32[2,4,3,2,1,512]{5,3,2,0,4,1:T(2,128)S(1)}, u32[]{:S(2)}, u32[]{:S(2)}) collective-permute-start(f32[2,4,3,2,1,512]{5,3,2,0,4,1:T(2,128)S(1)} %get-tuple-element.6), channel_id=1, source_target_pairs={{0,1},{1,2},{2,3},{3,4},{4,5},{5,6},{6,7},{7,8},{8,9},{9,10},{10,1... | collective-permute-start | bytes 294920 | tf_op jit(solution)/shard_map/ppermute | solution.py:30
  131.3 36.1 %collective-permute-start.9 = (f32[2,4,3,2,1,512]{5,3,2,0,4,1:T(2,128)S(1)}, f32[2,4,3,2,1,512]{5,3,2,0,4,1:T(2,128)S(1)}, u32[]{:S(2)}, u32[]{:S(2)}) collective-permute-start(f32[2,4,3,2,1,512]{5,3,2,0,4,1:T(2,128)S(1)} %get-tuple-element.6), channel_id=1, source_target_pairs={{1,0},{2,1},{3,2},{4,3},{5,4},{6,5},{7,6},{8,7},{9,8},{10,9},{11,1... | collective-permute-start | bytes 294920 | tf_op jit(solution)/shard_map/ppermute | solution.py:33
  145.1 15.5 %collective-permute-start.12 = (f32[1,2,3,2,1,512]{5,3,2,0,4,1:T(2,128)S(1)}, f32[1,2,3,2,1,512]{5,3,2,0,4,1:T(2,128)S(1)}, u32[]{:S(2)}, u32[]{:S(2)}) collective-permute-start(f32[1,2,3,2,1,512]{5,3,2,0,4,1:T(2,128)S(1)} %get-tuple-element.134), channel_id=1, source_target_pairs={{0,960},{64,0},{128,64},{192,128},{256,192},{320,256},{384,320},{4... | collective-permute-start | bytes 73736 | tf_op jit(solution)/shard_map/ppermute | solution.py:21
  150.0 17.3 %collective-permute-start.11 = (f32[1,2,3,2,1,512]{5,3,2,0,4,1:T(2,128)S(1)}, f32[1,2,3,2,1,512]{5,3,2,0,4,1:T(2,128)S(1)}, u32[]{:S(2)}, u32[]{:S(2)}) collective-permute-start(f32[1,2,3,2,1,512]{5,3,2,0,4,1:T(2,128)S(1)} %get-tuple-element.133), channel_id=1, source_target_pairs={{0,64},{64,128},{128,192},{192,256},{256,320},{320,384},{384,448},... | collective-permute-start | bytes 73736 | tf_op jit(solution)/shard_map/ppermute | solution.py:21
  168.6 20.6 %collective-permute-start.13 = (f32[2,4,3,2,1,512]{5,1,4,3,2,0:T(4,128)S(1)}, f32[2,4,3,2,1,512]{5,1,4,3,2,0:T(4,128)S(1)}, u32[]{:S(2)}, u32[]{:S(2)}) collective-permute-start(f32[2,4,3,2,1,512]{5,1,4,3,2,0:T(4,128)S(1)} %pad_maximum_fusion.1), channel_id=1, source_target_pairs={{0,64},{64,0},{128,192},{192,128},{256,320},{320,256},{384,448},{4... | collective-permute-start | bytes 294920 | tf_op jit(solution)/shard_map/ppermute | solution.py:41
  189.2 24.8 %collective-permute-start.14 = (f32[2,4,3,2,1,512]{5,1,4,3,2,0:T(4,128)S(1)}, f32[2,4,3,2,1,512]{5,1,4,3,2,0:T(4,128)S(1)}, u32[]{:S(2)}, u32[]{:S(2)}) collective-permute-start(f32[2,4,3,2,1,512]{5,1,4,3,2,0:T(4,128)S(1)} %collective-permute-done.13), channel_id=1, source_target_pairs={{0,128},{64,192},{128,0},{192,64},{256,384},{320,448},{384,256},{4... | collective-permute-start | bytes 294920 | tf_op jit(solution)/shard_map/ppermute | solution.py:41
  232.2 34.4 %collective-permute-start.18 = (f32[2,4,3,2,1,512]{5,3,2,0,4,1:T(2,128)S(1)}, f32[2,4,3,2,1,512]{5,3,2,0,4,1:T(2,128)S(1)}, u32[]{:S(2)}, u32[]{:S(2)}) collective-permute-start(f32[2,4,3,2,1,512]{5,3,2,0,4,1:T(2,128)S(1)} %copy.1596), channel_id=1, source_target_pairs={{0,1},{1,2},{2,3},{3,4},{4,5},{5,6},{6,7},{7,8},{8,9},{9,10},{10,1... | collective-permute-start | bytes 294920 | tf_op jit(solution)/shard_map/ppermute | solution.py:30
  234.2 32.6 %collective-permute-start.17 = (f32[2,4,3,2,1,512]{5,3,2,0,4,1:T(2,128)S(1)}, f32[2,4,3,2,1,512]{5,3,2,0,4,1:T(2,128)S(1)}, u32[]{:S(2)}, u32[]{:S(2)}) collective-permute-start(f32[2,4,3,2,1,512]{5,3,2,0,4,1:T(2,128)S(1)} %copy.1596), channel_id=1, source_target_pairs={{1,0},{2,1},{3,2},{4,3},{5,4},{6,5},{7,6},{8,7},{9,8},{10,9},{11,1... | collective-permute-start | bytes 294920 | tf_op jit(solution)/shard_map/ppermute | solution.py:33
  247.8 16.9 %collective-permute-start.19 = (f32[1,2,3,2,1,512]{5,3,2,0,4,1:T(2,128)S(1)}, f32[1,2,3,2,1,512]{5,3,2,0,4,1:T(2,128)S(1)}, u32[]{:S(2)}, u32[]{:S(2)}) collective-permute-start(f32[1,2,3,2,1,512]{5,3,2,0,4,1:T(2,128)S(1)} %get-tuple-element.106), channel_id=1, source_target_pairs={{0,64},{64,128},{128,192},{192,256},{256,320},{320,384},{384,448},... | collective-permute-start | bytes 73736 | tf_op jit(solution)/shard_map/ppermute | solution.py:21
  283.1 26.1 %collective-permute-start.22 = (f32[2,4,3,2,1,512]{5,1,4,3,2,0:T(4,128)S(1)}, f32[2,4,3,2,1,512]{5,1,4,3,2,0:T(4,128)S(1)}, u32[]{:S(2)}, u32[]{:S(2)}) collective-permute-start(f32[2,4,3,2,1,512]{5,1,4,3,2,0:T(4,128)S(1)} %collective-permute-done.21), channel_id=1, source_target_pairs={{0,128},{64,192},{128,0},{192,64},{256,384},{320,448},{384,256},{4... | collective-permute-start | bytes 294920 | tf_op jit(solution)/shard_map/ppermute | solution.py:41
  316.0 25.7 %collective-permute-start.24 = (f32[2,4,3,2,1,512]{5,1,4,3,2,0:T(4,128)S(1)}, f32[2,4,3,2,1,512]{5,1,4,3,2,0:T(4,128)S(1)}, u32[]{:S(2)}, u32[]{:S(2)}) collective-permute-start(f32[2,4,3,2,1,512]{5,1,4,3,2,0:T(4,128)S(1)} %collective-permute-done.23), channel_id=1, source_target_pairs={{0,512},{64,576},{128,640},{192,704},{256,768},{320,832},{384,896}... | collective-permute-start | bytes 294920 | tf_op jit(solution)/shard_map/ppermute | solution.py:41
  344.8 38.8 %collective-permute-start.26 = (f32[2,4,3,2,1,512]{5,3,2,0,4,1:T(2,128)S(1)}, f32[2,4,3,2,1,512]{5,3,2,0,4,1:T(2,128)S(1)}, u32[]{:S(2)}, u32[]{:S(2)}) collective-permute-start(f32[2,4,3,2,1,512]{5,3,2,0,4,1:T(2,128)S(1)} %copy.1752), channel_id=1, source_target_pairs={{0,1},{1,2},{2,3},{3,4},{4,5},{5,6},{6,7},{7,8},{8,9},{9,10},{10,1... | collective-permute-start | bytes 294920 | tf_op jit(solution)/shard_map/ppermute | solution.py:30
  346.7 37.2 %collective-permute-start.25 = (f32[2,4,3,2,1,512]{5,3,2,0,4,1:T(2,128)S(1)}, f32[2,4,3,2,1,512]{5,3,2,0,4,1:T(2,128)S(1)}, u32[]{:S(2)}, u32[]{:S(2)}) collective-permute-start(f32[2,4,3,2,1,512]{5,3,2,0,4,1:T(2,128)S(1)} %copy.1752), channel_id=1, source_target_pairs={{1,0},{2,1},{3,2},{4,3},{5,4},{6,5},{7,6},{8,7},{9,8},{10,9},{11,1... | collective-permute-start | bytes 294920 | tf_op jit(solution)/shard_map/ppermute | solution.py:33
  361.7 21.7 %collective-permute-start.27 = (f32[1,2,3,2,1,512]{5,3,2,0,4,1:T(2,128)S(1)}, f32[1,2,3,2,1,512]{5,3,2,0,4,1:T(2,128)S(1)}, u32[]{:S(2)}, u32[]{:S(2)}) collective-permute-start(f32[1,2,3,2,1,512]{5,3,2,0,4,1:T(2,128)S(1)} %get-tuple-element.83), channel_id=1, source_target_pairs={{0,64},{64,128},{128,192},{192,256},{256,320},{320,384},{384,448},... | collective-permute-start | bytes 73736 | tf_op jit(solution)/shard_map/ppermute | solution.py:21
  363.7 19.8 %collective-permute-start.28 = (f32[1,2,3,2,1,512]{5,1,4,3,2,0:T(2,128)S(1)}, f32[1,2,3,2,1,512]{5,1,4,3,2,0:T(2,128)S(1)}, u32[]{:S(2)}, u32[]{:S(2)}) collective-permute-start(f32[1,2,3,2,1,512]{5,1,4,3,2,0:T(2,128)S(1)} %get-tuple-element.86), channel_id=1, source_target_pairs={{0,960},{64,0},{128,64},{192,128},{256,192},{320,256},{384,320},{4... | collective-permute-start | bytes 73736 | tf_op jit(solution)/shard_map/ppermute | solution.py:21
  384.7 18.5 %collective-permute-start.29 = (f32[2,4,3,2,1,512]{5,1,4,3,2,0:T(4,128)S(1)}, f32[2,4,3,2,1,512]{5,1,4,3,2,0:T(4,128)S(1)}, u32[]{:S(2)}, u32[]{:S(2)}) collective-permute-start(f32[2,4,3,2,1,512]{5,1,4,3,2,0:T(4,128)S(1)} %pad_maximum_fusion.3), channel_id=1, source_target_pairs={{0,64},{64,0},{128,192},{192,128},{256,320},{320,256},{384,448},{4... | collective-permute-start | bytes 294920 | tf_op jit(solution)/shard_map/ppermute | solution.py:41
  403.2 24.8 %collective-permute-start.30 = (f32[2,4,3,2,1,512]{5,1,4,3,2,0:T(4,128)S(1)}, f32[2,4,3,2,1,512]{5,1,4,3,2,0:T(4,128)S(1)}, u32[]{:S(2)}, u32[]{:S(2)}) collective-permute-start(f32[2,4,3,2,1,512]{5,1,4,3,2,0:T(4,128)S(1)} %collective-permute-done.29), channel_id=1, source_target_pairs={{0,128},{64,192},{128,0},{192,64},{256,384},{320,448},{384,256},{4... | collective-permute-start | bytes 294920 | tf_op jit(solution)/shard_map/ppermute | solution.py:41
  (10 other events, 96.9 us)
where the time goes:
time: 444 us; the launch traced here: 443 us
  starting transfers between devices  228 us (51%)
  waiting for transfers between devices  180 us (41%)
  other arithmetic  24.4 us (5%)
  local copies, waits for them, and re-layouts  5.55 us (1%)
  between operations  4.96 us (1%)
    ppermute x16, waiting for transfers between devices, swapped(): return lax.ppermute(value, axis, pairs)  160 us
    ppermute x16, starting transfers between devices, swapped(): return lax.ppermute(value, axis, pairs)  104 us
    ppermute x9, starting transfers between devices, shifted(): return lax.ppermute(value, axis, pairs)  65 us
    ppermute x4, starting transfers between devices, padded_2(): lax.ppermute(lax.slice_in_dim(block, 0, width, axis=dim), axis, backward)  52 us
    ppermute x9, waiting for transfers between devices, shifted(): return lax.ppermute(value, axis, pairs)  20.1 us
  transfers between devices with their start and end apart: 33, of which 20 were waited for; matrix products, arithmetic and copies ran while one was open for 3% of the time, Pallas kernels for 0%

commit v1 on v0

v1 whole, which is shorter than its diff:
```python
import functools

import jax
import jax.numpy as jnp
from jax import lax
from jax.experimental import pallas as pl
from jax.experimental.pallas import tpu as pltpu
from jax.sharding import PartitionSpec as P

MESH = pl.DeviceIdType.MESH
wall_height = 1.8
quark_mass = 0.1
filter_center = 0.5
filter_radius = 8.0
DEGREE = 4
gamma_block = (((1, 1), (0, 1)), ((1, 2), (0, 0)), ((0, 1), (1, 3)), ((0, 0), (1, 0)))
gamma_adjoint = (((1, 3), (0, 3)), ((1, 0), (0, 2)), ((0, 3), (1, 1)), ((0, 0), (1, 0)))
NX, NY, NHI, NC = 4, 4, 4, 2
TP, TM, KP, KM, SP, SM = range(6)


def unit_part(quarter, part):
    if part == 0:
        return ((1.0, 0), (-1.0, 1), (-1.0, 0), (1.0, 1))[quarter]
    return ((1.0, 1), (1.0, 0), (-1.0, 1), (-1.0, 0))[quarter]


def plus(value, sign, term):
    return value + term if sign > 0 else value - term


def comp(spin, colour, part):
    return (spin * 3 + colour) * 2 + part


def project(field, direction, parity):
    half = []
    for row in range(2):
        source, quarter = gamma_block[direction][row]
        for colour in range(3):
            for part in range(2):
                sign, other = unit_part(quarter, part)
                half.append(
                    plus(field(comp(row, colour, part)), parity * sign, field(comp(2 + source, colour, other)))
                )
    return half


def add_rebuilt(total, half, direction, parity):
    for row in range(2):
        source, quarter = gamma_adjoint[direction][row]
        for colour in range(3):
            for part in range(2):
                n = comp(row, colour, part)
                total[n] = total[n] + half[n]
                sign, other = unit_part(quarter, part)
                m = comp(2 + row, colour, part)
                total[m] = plus(total[m], parity * sign, half[comp(source, colour, other)])


def colour_mul(link, half, dagger):
    result = [None] * 12
    for row in range(3):
        for column in range(3):
            if dagger:
                u_re, u_im, sign = link(column, row, 0), link(column, row, 1), -1.0
            else:
                u_re, u_im, sign = link(row, column, 0), link(row, column, 1), 1.0
            for spin in range(2):
                h_re, h_im = half[comp(spin, column, 0)], half[comp(spin, column, 1)]
                re = plus(u_re * h_re, -sign, u_im * h_im)
                im = plus(u_re * h_im, sign, u_im * h_re)
                r, i = comp(spin, row, 0), comp(spin, row, 1)
                result[r] = re if column == 0 else result[r] + re
                result[i] = im if column == 0 else result[i] + im
    return result


def kernel(
    nlo,
    sp_ref,
    g_ref,
    out_ref,
    stage,
    gstage,
    psi_in,
    g_in,
    links,
    field,
    tsend,
    trecv,
    ksend,
    krecv,
    klocal,
    ssend,
    srecv,
    ostage,
    o_in,
    send1,
    recv1,
    sendg,
    recvg,
    sendh,
    recvh,
    send2,
    recv2,
    local,
):
    nz = NHI * nlo
    nt = nz * NC
    f = lax.axis_index("fifth")
    p = lax.axis_index("space")
    y, zhi = lax.div(f, NHI), lax.rem(f, NHI)
    zlo, x, c = lax.div(p, NX * NC), lax.rem(lax.div(p, NC), NX), lax.rem(p, NC)
    z = zhi * nlo + zlo

    def device(dx, dy, dz, dc):
        return (dy * NHI + lax.div(dz, nlo), lax.rem(dz, nlo) * (NX * NC) + dx * NC + dc)

    z_to = lax.div(p, NC)
    upper = f >= 8
    folded = jnp.where(upper, 15 - f, f)
    y_to = lax.div(folded, 2)
    slot = jnp.where(upper, 2, 0) + lax.rem(folded, 2)
    flip = jnp.where(upper, 1, 0)
    ahead = lax.rem(z_to - zlo + nz, nz)
    gives_links = zhi == lax.rem(lax.div(ahead + nlo // 2, nlo), NHI)
    to_self = (y_to == y) & (z_to == z)
    t = z * NC + c
    sources = (2 * y, 2 * y + 1, 15 - 2 * y, 14 - 2 * y)
    ahead_me = lax.rem(z - lax.div(t, NX * NC) + nz, nz)
    link_hi = lax.rem(lax.div(ahead_me + nlo // 2, nlo), NHI)

    t_up, t_down = lax.rem(t + 1, nt), lax.rem(t + nt - 1, nt)
    near = {
        TP: device(x, y, lax.div(t_up, NC), lax.rem(t_up, NC)),
        TM: device(x, y, lax.div(t_down, NC), lax.rem(t_down, NC)),
        KP: device(lax.rem(x + 1, NX), y, z, c),
        KM: device(lax.rem(x + NX - 1, NX), y, z, c),
        SP: device(x, jnp.minimum(y + 1, NY - 1), z, c),
        SM: device(x, jnp.maximum(y - 1, 0), z, c),
    }

    barrier = pltpu.get_barrier_semaphore()

    def greet(device_id):
        pl.semaphore_signal(barrier, inc=1, device_id=device_id, device_id_type=MESH)

    for q in range(NX):

        @pl.when(jnp.logical_not(to_self & (x == q)))
        def _():
            greet(device(q, y_to, z_to, c))

    for n in range(4):

        @pl.when(jnp.logical_not(to_self & (slot == n)))
        def _():
            greet((sources[n], t))

    for side in (TP, TM, KP, KM):
        greet(near[side])

    @pl.when(y < NY - 1)
    def _():
        greet(near[SP])

    @pl.when(y > 0)
    def _():
        greet(near[SM])

    for q in range(NX):
        for s in range(2):
            for b in range(3):
                row = pl.multiple_of(q * 48 + lax.rem(s + flip, 2) * 24 + b * 8, 8)
                stage[pl.ds(row, 8), :] = sp_ref[pl.ds((s * 24 + b * 8) * 4 + q, 8, stride=4), :]
        for mu in range(4):
            first = g_ref[pl.ds(mu * 72 + q, 8, stride=4), :]
            gstage[q * 48 + mu * 12 : q * 48 + mu * 12 + 8, :] = first
            last = g_ref[pl.ds(mu * 72 + 32 + q, 4, stride=4), :]
            gstage[q * 48 + mu * 12 + 8 : q * 48 + mu * 12 + 12, :] = last

    count = 12 - jnp.where(to_self, 2, 0) + jnp.where(y > 0, 1, 0) + jnp.where(y < NY - 1, 1, 0)
    pl.semaphore_wait(barrier, count)

    def block(ref, n):
        start = n * 48
        return ref.at[pl.ds(start if isinstance(n, int) else pl.multiple_of(start, 8), 48), :]

    def out_copy(q):
        return pltpu.make_async_remote_copy(
            src_ref=block(stage, q),
            dst_ref=block(psi_in, slot),
            send_sem=send1.at[q],
            recv_sem=recv1.at[slot],
            device_id=device(q, y_to, z_to, c),
            device_id_type=MESH,
        )

    def link_copy(q):
        return pltpu.make_async_remote_copy(
            src_ref=block(gstage, q),
            dst_ref=g_in,
            send_sem=sendg.at[q],
            recv_sem=recvg.at[0],
            device_id=device(q, y_to, z_to, c),
            device_id_type=MESH,
        )

    for q in range(NX):
        other = jnp.logical_not(to_self & (x == q))

        @pl.when(other)
        def _():
            out_copy(q).start()

        @pl.when(other & gives_links)
        def _():
            link_copy(q).start()

    @pl.when(to_self)
    def _():
        mine = pltpu.make_async_copy(block(stage, x), block(psi_in, slot), local.at[0])
        mine.start()
        mine.wait()

    @pl.when(to_self & gives_links)
    def _():
        mine = pltpu.make_async_copy(block(gstage, x), g_in, local.at[1])
        mine.start()
        mine.wait()

    for n in range(24):
        field[0, n] = jnp.zeros((8, 128), jnp.float32)

    @pl.when(jnp.logical_not(to_self & (zhi == link_hi)))
    def _():
        link_copy(0).wait_recv()

    for mu in range(4):
        scale = -0.5 / filter_radius
        if mu == 3:
            scale = scale * jnp.where(t == nt - 1, -1.0, 1.0)
        rows = [
            jnp.broadcast_to(g_in[mu * 12 + r : mu * 12 + r + 1, :], (8, 128)) for r in range(12)
        ]
        for r in range(12):
            links[mu * 18 + r] = rows[r] * scale
        for i in range(3):
            j, k = (i + 1) % 3, (i + 2) % 3
            a_re, a_im, b_re, b_im = rows[2 * j], rows[2 * j + 1], rows[6 + 2 * k], rows[7 + 2 * k]
            c_re, c_im, d_re, d_im = rows[2 * k], rows[2 * k + 1], rows[6 + 2 * j], rows[7 + 2 * j]
            re = (a_re * b_re - a_im * b_im) - (c_re * d_re - c_im * d_im)
            im = (c_re * d_im + c_im * d_re) - (a_re * b_im + a_im * b_re)
            links[mu * 18 + 12 + 2 * i] = re * scale
            links[mu * 18 + 13 + 2 * i] = im * scale

    for n in range(4):

        @pl.when(jnp.logical_not(to_self & (slot == n)))
        def _():
            pltpu.make_async_remote_copy(
                src_ref=block(stage, 0),
                dst_ref=block(psi_in, n),
                send_sem=send1.at[0],
                recv_sem=recv1.at[n],
                device_id=near[TP],
                device_id_type=MESH,
            ).wait_recv()

    for n in range(24):
        field[1, n] = psi_in[pl.ds(n, 8, stride=24), :]

    lane = lax.broadcasted_iota(jnp.int32, (8, 128), 1)
    sub = lax.broadcasted_iota(jnp.int32, (8, 128), 0)
    low = lane < 64

    def shift(value, direction, forward):
        stride = 8**direction
        position = lax.rem(lax.div(lane, stride), 8)
        inside, outside = (128 - stride, 7 * stride) if forward else (stride, 128 - 7 * stride)
        edge = position == (7 if forward else 0)
        return jnp.where(edge, pltpu.roll(value, outside, 1), pltpu.roll(value, inside, 1))

    def half_turn(value):
        return pltpu.roll(value, 64, 1)

    def step(it, carry):
        def v(n):
            return field[it + 1, n]

        def link(mu):
            return lambda row, column, part: links[mu * 18 + (row * 3 + column) * 2 + part]

        def halo(side, source, target):
            return pltpu.make_async_remote_copy(
                src_ref=source,
                dst_ref=target,
                send_sem=sendh.at[it, side],
                recv_sem=recvh.at[it, side],
                device_id=near[side],
                device_id_type=MESH,
            )

        to_t_up = halo(TP, tsend.at[it, 0], trecv.at[it, 0])
        to_t_down = halo(TM, tsend.at[it, 1], trecv.at[it, 1])
        to_k_up = halo(KP, ksend.at[it, 0], krecv.at[it, 0])
        to_k_down = halo(KM, ksend.at[it, 1], krecv.at[it, 1])
        to_s_up = halo(SP, ssend.at[it, 0], srecv.at[it, 0])
        to_s_down = halo(SM, ssend.at[it, 1], srecv.at[it, 1])

        behind = colour_mul(link(3), project(v, 3, 1.0), True)
        for n in range(12):
            tsend[it, 0, n] = behind[n]
        to_t_up.start()
        front = project(v, 3, -1.0)
        for n in range(12):
            tsend[it, 1, n] = front[n]
        to_t_down.start()

        behind = colour_mul(link(2), project(v, 2, 1.0), True)
        for m in range(6):
            a, b = behind[2 * m], behind[2 * m + 1]
            ra, rb = half_turn(a), half_turn(b)
            ksend[it, 0, m] = jnp.where(low, ra, b)
            klocal[0, 2 * m] = ra
            klocal[0, 2 * m + 1] = rb
        to_k_up.start()
        front = project(v, 2, -1.0)
        for m in range(6):
            a, b = front[2 * m], front[2 * m + 1]
            ra, rb = half_turn(a), half_turn(b)
            ksend[it, 1, m] = jnp.where(low, a, rb)
            klocal[1, 2 * m] = ra
            klocal[1, 2 * m + 1] = rb
        to_k_down.start()

        for n in range(24):
            value = v(n)
            up, down = (3, 4) if n < 12 else (7, 0)
            ssend[it, 0, n : n + 1] = value[up : up + 1]
            ssend[it, 1, n : n + 1] = value[down : down + 1]

        @pl.when(y < NY - 1)
        def _():
            to_s_up.start()

        @pl.when(y > 0)
        def _():
            to_s_down.start()

        @pl.when(y == NY - 1)
        def _():
            srecv[it, 1] = ssend[it, 0]

        @pl.when(y == 0)
        def _():
            srecv[it, 0] = ssend[it, 1] * -quark_mass

        total = [((5.0 - wall_height) / filter_radius) * v(n) for n in range(24)]
        for direction in range(2):
            front = [shift(value, direction, True) for value in project(v, direction, -1.0)]
            add_rebuilt(total, colour_mul(link(direction), front, False), direction, -1.0)
            behind = colour_mul(link(direction), project(v, direction, 1.0), True)
            add_rebuilt(total, [shift(value, direction, False) for value in behind], direction, 1.0)

        to_k_up.wait_recv()
        behind = []
        for m in range(6):
            packed = krecv[it, 0, m]
            behind.append(jnp.where(low, packed, klocal[0, 2 * m]))
            behind.append(jnp.where(low, half_turn(packed), klocal[0, 2 * m + 1]))
        add_rebuilt(total, behind, 2, 1.0)
        to_k_down.wait_recv()
        front = []
        for m in range(6):
            packed = krecv[it, 1, m]
            front.append(jnp.where(low, klocal[1, 2 * m], half_turn(packed)))
            front.append(jnp.where(low, klocal[1, 2 * m + 1], packed))
        add_rebuilt(total, colour_mul(link(2), front, False), 2, -1.0)

        @pl.when(y > 0)
        def _():
            to_s_up.wait_recv()

        @pl.when(y < NY - 1)
        def _():
            to_s_down.wait_recv()

        for n in range(24):
            value = v(n)
            back, on = pltpu.roll(value, 1, 0), pltpu.roll(value, 7, 0)
            from_low = jnp.broadcast_to(srecv[it, 0, n : n + 1], (8, 128))
            from_high = jnp.broadcast_to(srecv[it, 1, n : n + 1], (8, 128))
            if n < 12:
                inner = jnp.where(sub < 4, back, on)
                moved = jnp.where(sub == 0, from_low, jnp.where(sub == 7, from_high, inner))
            else:
                inner = jnp.where(sub < 4, on, back)
                moved = jnp.where(sub == 4, from_low, jnp.where(sub == 3, from_high, inner))
            total[n] = total[n] - (1.0 / filter_radius) * moved

        to_t_up.wait_recv()
        add_rebuilt(total, [trecv[it, 0, n] for n in range(12)], 3, 1.0)
        to_t_down.wait_recv()
        front = [trecv[it, 1, n] for n in range(12)]
        add_rebuilt(total, colour_mul(link(3), front, False), 3, -1.0)

        gain = jnp.where(it == 0, 1.0, 2.0)
        for n in range(24):
            signed = pltpu.roll(total[n], 4, 0)
            centred = (filter_center / filter_radius) * v(n)
            inner = (signed if n < 12 else -signed) - centred
            field[it + 2, n] = gain * inner - field[it, n]
        return carry

    lax.fori_loop(0, DEGREE, step, 0)

    for n in range(24):
        ostage[pl.ds(n, 8, stride=24), :] = field[DEGREE + 1, n]

    def back_copy(n):
        return pltpu.make_async_remote_copy(
            src_ref=block(ostage, n),
            dst_ref=block(o_in, x),
            send_sem=send2.at[n],
            recv_sem=recv2.at[x],
            device_id=(sources[n], t),
            device_id_type=MESH,
        )

    for n in range(4):

        @pl.when(jnp.logical_not(to_self & (slot == n)))
        def _():
            back_copy(n).start()

    @pl.when(to_self)
    def _():
        mine = pltpu.make_async_copy(block(ostage, slot), block(o_in, x), local.at[0])
        mine.start()
        mine.wait()

    for q in range(NX):

        @pl.when(jnp.logical_not(to_self & (x == q)))
        def _():
            pltpu.make_async_remote_copy(
                src_ref=block(ostage, 0),
                dst_ref=block(o_in, q),
                send_sem=send2.at[0],
                recv_sem=recv2.at[q],
                device_id=near[TP],
                device_id_type=MESH,
            ).wait_recv()

        for s in range(2):
            for b in range(3):
                row = pl.multiple_of(q * 48 + lax.rem(s + flip, 2) * 24 + b * 8, 8)
                out_ref[pl.ds((s * 24 + b * 8) * 4 + q, 8, stride=4), :] = o_in[pl.ds(row, 8), :]

    for q in range(NX):
        other = jnp.logical_not(to_self & (x == q))

        @pl.when(other)
        def _():
            out_copy(q).wait_send()

        @pl.when(other & gives_links)
        def _():
            link_copy(q).wait_send()

    def sent(it, carry):
        def left(side, source, target):
            pltpu.make_async_remote_copy(
                src_ref=source,
                dst_ref=target,
                send_sem=sendh.at[it, side],
                recv_sem=recvh.at[it, side],
                device_id=near[side],
                device_id_type=MESH,
            ).wait_send()

        left(TP, tsend.at[it, 0], trecv.at[it, 0])
        left(TM, tsend.at[it, 1], trecv.at[it, 1])
        left(KP, ksend.at[it, 0], krecv.at[it, 0])
        left(KM, ksend.at[it, 1], krecv.at[it, 1])

        @pl.when(y < NY - 1)
        def _():
            left(SP, ssend.at[it, 0], srecv.at[it, 0])

        @pl.when(y > 0)
        def _():
            left(SM, ssend.at[it, 1], srecv.at[it, 1])

        return carry

    lax.fori_loop(0, DEGREE, sent, 0)

    for n in range(4):

        @pl.when(jnp.logical_not(to_self & (slot == n)))
        def _():
            back_copy(n).wait_send()


def solution(mesh):
    nlo = mesh.shape["space"] // (NX * NC)
    vmem = pl.BlockSpec(memory_space=pltpu.VMEM)

    def f32(*shape):
        return pltpu.VMEM(shape, jnp.float32)

    dma = pltpu.SemaphoreType.DMA

    def on_device(spinor, gauge_links):
        out = pl.pallas_call(
            functools.partial(kernel, nlo),
            out_shape=jax.ShapeDtypeStruct((192, 128), jnp.float32),
            in_specs=[vmem, vmem],
            out_specs=vmem,
            scratch_shapes=[
                f32(192, 128),
                f32(192, 128),
                f32(192, 128),
                f32(48, 128),
                f32(72, 8, 128),
                f32(DEGREE + 2, 24, 8, 128),
                f32(DEGREE, 2, 12, 8, 128),
                f32(DEGREE, 2, 12, 8, 128),
                f32(DEGREE, 2, 6, 8, 128),
                f32(DEGREE, 2, 6, 8, 128),
                f32(2, 12, 8, 128),
                f32(DEGREE, 2, 24, 128),
                f32(DEGREE, 2, 24, 128),
                f32(192, 128),
                f32(192, 128),
                dma((4,)),
                dma((4,)),
                dma((4,)),
                dma((1,)),
                dma((DEGREE, 6)),
                dma((DEGREE, 6)),
                dma((4,)),
                dma((4,)),
                dma((2,)),
            ],
            compiler_params=pltpu.CompilerParams(
                collective_id=0, has_side_effects=True, vmem_limit_bytes=16 * 2**20
            ),
        )(spinor.reshape(192, 128), gauge_links.reshape(288, 128))
        return out.reshape(2, 24, 1, 512)

    return jax.shard_map(
        on_device,
        mesh=mesh,
        in_specs=(P("fifth", None, "space", None), P(None, None, "space", None)),
        out_specs=P("fifth", None, "space", None),
        check_vma=False,
    )
```

time: 444 us -> 85.3 us (0.19)
  the two profiles are of different devices: /device:TPU:8 before, /device:TPU:154 now
where the time goes in v1:
time: 85.3 us; the launch traced here: 85.1 us
  Pallas kernels  82.7 us (97%)
  local copies, waits for them, and re-layouts  2.44 us (3%)
    pallas_call x1, Pallas kernels, on_device(): pl.pallas_call(functools.partial(kernel, nlo), out_shape=jax.ShapeDtypeSt...  82.7 us
    unnamed x5, local copies, waits for them, and re-layouts  2.44 us

profile of v1, /device:TPU:154, one launch (start us, length us, event | category | flops | bytes accessed | tf_op | source)
XLA Modules:
  0.0 85.1 jit_solution(11523099019191832475)
XLA Ops:
  0.0 0.0 copy-start
  0.0 0.9 %copy-done = f32[4,18,1,512]{3,2,1,0:T(1,128)S(1)} copy-done((f32[4,18,1,512]{3,2,1,0:T(1,128)S(1)}, f32[4,18,1,512]{3,2,1,0:T(1,128)}, u32[]{:S(2)}) %copy-start) | copy-done | bytes 147480
  0.9 0.0 copy-start.1
  0.9 0.9 %copy-done.1 = f32[2,24,1,512]{3,2,1,0:T(1,128)S(1)} copy-done((f32[2,24,1,512]{3,2,1,0:T(1,128)S(1)}, f32[2,24,1,512]{3,2,1,0:T(1,128)}, u32[]{:S(2)}) %copy-start.1) | copy-done | bytes 98328
  1.8 82.7 %shard_map.28 = f32[192,128]{1,0:T(8,128)S(1)} custom-call(f32[192,128]{1,0:T(8,128)S(1)} %bitcast.5, f32[288,128]{1,0:T(8,128)S(1)} %bitcast.4), custom_call_target="tpu_custom_call" | custom-call | tf_op jit(solution)/shard_map/pallas_call | solution.py:518
  84.5 0.6 copy.5
Async XLA Ops:
  0.0 0.9 %copy-start = (f32[4,18,1,512]{3,2,1,0:T(1,128)S(1)}, f32[4,18,1,512]{3,2,1,0:T(1,128)}, u32[]{:S(2)}) copy-start(f32[4,18,1,512]{3,2,1,0:T(1,128)} %param.3) | copy-start | bytes 442372
  0.9 0.9 %copy-start.1 = (f32[2,24,1,512]{3,2,1,0:T(1,128)S(1)}, f32[2,24,1,512]{3,2,1,0:T(1,128)}, u32[]{:S(2)}) copy-start(f32[2,24,1,512]{3,2,1,0:T(1,128)} %param.2) | copy-start | bytes 294916

commit v2 on v1

--- a/solution.py
+++ b/solution.py
@@ -16,6 +16,7 @@
 gamma_block = (((1, 1), (0, 1)), ((1, 2), (0, 0)), ((0, 1), (1, 3)), ((0, 0), (1, 0)))
 gamma_adjoint = (((1, 3), (0, 3)), ((1, 0), (0, 2)), ((0, 3), (1, 1)), ((0, 0), (1, 0)))
 NX, NY, NHI, NC = 4, 4, 4, 2
+Z_OFFSET = 28
 TP, TM, KP, KM, SP, SM = range(6)
 
 
@@ -78,9 +79,11 @@
 
 def kernel(
     nlo,
+    sp_hbm,
+    g_hbm,
+    out_ref,
     sp_ref,
     g_ref,
-    out_ref,
     stage,
     gstage,
     psi_in,
@@ -117,28 +120,29 @@
     def device(dx, dy, dz, dc):
         return (dy * NHI + lax.div(dz, nlo), lax.rem(dz, nlo) * (NX * NC) + dx * NC + dc)
 
-    z_to = lax.div(p, NC)
+    z_to = lax.rem(lax.div(p, NC) + Z_OFFSET, nz)
     upper = f >= 8
     folded = jnp.where(upper, 15 - f, f)
-    y_to = lax.div(folded, 2)
+    y_to = lax.rem(NY - lax.div(folded, 2), NY)
     slot = jnp.where(upper, 2, 0) + lax.rem(folded, 2)
     flip = jnp.where(upper, 1, 0)
     ahead = lax.rem(z_to - zlo + nz, nz)
     gives_links = zhi == lax.rem(lax.div(ahead + nlo // 2, nlo), NHI)
     to_self = (y_to == y) & (z_to == z)
-    t = z * NC + c
-    sources = (2 * y, 2 * y + 1, 15 - 2 * y, 14 - 2 * y)
+    t = lax.rem(z + nz - Z_OFFSET % nz, nz) * NC + c
+    seg = lax.rem(NY - y, NY)
+    sources = (2 * seg, 2 * seg + 1, 15 - 2 * seg, 14 - 2 * seg)
     ahead_me = lax.rem(z - lax.div(t, NX * NC) + nz, nz)
     link_hi = lax.rem(lax.div(ahead_me + nlo // 2, nlo), NHI)
 
     t_up, t_down = lax.rem(t + 1, nt), lax.rem(t + nt - 1, nt)
     near = {
-        TP: device(x, y, lax.div(t_up, NC), lax.rem(t_up, NC)),
-        TM: device(x, y, lax.div(t_down, NC), lax.rem(t_down, NC)),
+        TP: device(x, y, lax.rem(lax.div(t_up, NC) + Z_OFFSET, nz), lax.rem(t_up, NC)),
+        TM: device(x, y, lax.rem(lax.div(t_down, NC) + Z_OFFSET, nz), lax.rem(t_down, NC)),
         KP: device(lax.rem(x + 1, NX), y, z, c),
         KM: device(lax.rem(x + NX - 1, NX), y, z, c),
-        SP: device(x, jnp.minimum(y + 1, NY - 1), z, c),
-        SM: device(x, jnp.maximum(y - 1, 0), z, c),
+        SP: device(x, lax.rem(y + NY - 1, NY), z, c),
+        SM: device(x, lax.rem(y + 1, NY), z, c),
     }
 
     barrier = pltpu.get_barrier_semaphore()
@@ -146,12 +150,6 @@
     def greet(device_id):
         pl.semaphore_signal(barrier, inc=1, device_id=device_id, device_id_type=MESH)
 
-    for q in range(NX):
-
-        @pl.when(jnp.logical_not(to_self & (x == q)))
-        def _():
-            greet(device(q, y_to, z_to, c))
-
     for n in range(4):
 
         @pl.when(jnp.logical_not(to_self & (slot == n)))
@@ -161,13 +159,18 @@
     for side in (TP, TM, KP, KM):
         greet(near[side])
 
-    @pl.when(y < NY - 1)
+    @pl.when(seg < NY - 1)
     def _():
         greet(near[SP])
 
-    @pl.when(y > 0)
+    @pl.when(seg > 0)
     def _():
         greet(near[SM])
+
+    for source, target, sem in ((sp_hbm, sp_ref, 2), (g_hbm, g_ref, 3)):
+        pltpu.make_async_copy(source, target, local.at[sem]).start()
+    pltpu.make_async_copy(sp_hbm, sp_ref, local.at[2]).wait()
+    pltpu.make_async_copy(g_hbm, g_ref, local.at[3]).wait()
 
     for q in range(NX):
         for s in range(2):
@@ -180,7 +183,7 @@
             last = g_ref[pl.ds(mu * 72 + 32 + q, 4, stride=4), :]
             gstage[q * 48 + mu * 12 + 8 : q * 48 + mu * 12 + 12, :] = last
 
-    count = 12 - jnp.where(to_self, 2, 0) + jnp.where(y > 0, 1, 0) + jnp.where(y < NY - 1, 1, 0)
+    count = 8 - jnp.where(to_self, 1, 0) + jnp.where(seg > 0, 1, 0) + jnp.where(seg < NY - 1, 1, 0)
     pl.semaphore_wait(barrier, count)
 
     def block(ref, n):
@@ -341,19 +344,19 @@
             ssend[it, 0, n : n + 1] = value[up : up + 1]
             ssend[it, 1, n : n + 1] = value[down : down + 1]
 
-        @pl.when(y < NY - 1)
+        @pl.when(seg < NY - 1)
         def _():
             to_s_up.start()
 
-        @pl.when(y > 0)
+        @pl.when(seg > 0)
         def _():
             to_s_down.start()
 
-        @pl.when(y == NY - 1)
+        @pl.when(seg == NY - 1)
         def _():
             srecv[it, 1] = ssend[it, 0]
 
-        @pl.when(y == 0)
+        @pl.when(seg == 0)
         def _():
             srecv[it, 0] = ssend[it, 1] * -quark_mass
 
@@ -379,11 +382,11 @@
             front.append(jnp.where(low, klocal[1, 2 * m + 1], packed))
         add_rebuilt(total, colour_mul(link(2), front, False), 2, -1.0)
 
-        @pl.when(y > 0)
+        @pl.when(seg > 0)
         def _():
             to_s_up.wait_recv()
 
-        @pl.when(y < NY - 1)
+        @pl.when(seg < NY - 1)
         def _():
             to_s_down.wait_recv()
 
@@ -429,11 +432,20 @@
             device_id_type=MESH,
         )
 
-    for n in range(4):
-
-        @pl.when(jnp.logical_not(to_self & (slot == n)))
-        def _():
-            back_copy(n).start()
+    for early in (True, False):
+        for n in range(4):
+            first = (lax.rem(sources[n], NHI) < 2) if early else (lax.rem(sources[n], NHI) >= 2)
+
+            @pl.when(jnp.logical_not(to_self & (slot == n)) & first)
+            def _():
+                back_copy(n).start()
+
+        if early:
+            for n in range(4):
+
+                @pl.when(jnp.logical_not(to_self & (slot == n)) & (lax.rem(sources[n], NHI) < 2))
+                def _():
+                    back_copy(n).wait_send()
 
     @pl.when(to_self)
     def _():
@@ -486,11 +498,11 @@
         left(KP, ksend.at[it, 0], krecv.at[it, 0])
         left(KM, ksend.at[it, 1], krecv.at[it, 1])
 
-        @pl.when(y < NY - 1)
+        @pl.when(seg < NY - 1)
         def _():
             left(SP, ssend.at[it, 0], srecv.at[it, 0])
 
-        @pl.when(y > 0)
+        @pl.when(seg > 0)
         def _():
             left(SM, ssend.at[it, 1], srecv.at[it, 1])
 
@@ -500,7 +512,7 @@
 
     for n in range(4):
 
-        @pl.when(jnp.logical_not(to_self & (slot == n)))
+        @pl.when(jnp.logical_not(to_self & (slot == n)) & (lax.rem(sources[n], NHI) >= 2))
         def _():
             back_copy(n).wait_send()
 
@@ -518,9 +530,11 @@
         out = pl.pallas_call(
             functools.partial(kernel, nlo),
             out_shape=jax.ShapeDtypeStruct((192, 128), jnp.float32),
-            in_specs=[vmem, vmem],
+            in_specs=[pl.BlockSpec(memory_space=pl.ANY)] * 2,
             out_specs=vmem,
             scratch_shapes=[
+                f32(192, 128),
+                f32(288, 128),
                 f32(192, 128),
                 f32(192, 128),
                 f32(192, 128),
@@ -544,10 +558,10 @@
                 dma((DEGREE, 6)),
                 dma((4,)),
                 dma((4,)),
-                dma((2,)),
+                dma((4,)),
             ],
             compiler_params=pltpu.CompilerParams(
-                collective_id=0, has_side_effects=True, vmem_limit_bytes=16 * 2**20
+                collective_id=0, has_side_effects=True, vmem_limit_bytes=60 * 2**20
             ),
         )(spinor.reshape(192, 128), gauge_links.reshape(288, 128))
         return out.reshape(2, 24, 1, 512)

time: 85.3 us -> 80.6 us (0.945)
  the two profiles are of different devices: /device:TPU:154 before, /device:TPU:160 now
where the time goes in v2:
time: 80.6 us; the launch traced here: 80.4 us
  Pallas kernels  78.9 us (98%)
  local copies, waits for them, and re-layouts  1.54 us (2%)
    pallas_call x1, Pallas kernels, on_device(): pl.pallas_call(functools.partial(kernel, nlo), out_shape=jax.ShapeDtypeSt...  78.9 us

profile of v2, /device:TPU:160, one launch (start us, length us, event | category | flops | bytes accessed | tf_op | source)
XLA Modules:
  0.0 80.4 jit_solution(10021468463516958392)
XLA Ops:
  0.0 78.9 %shard_map.28 = f32[192,128]{1,0:T(8,128)} custom-call(f32[192,128]{1,0:T(8,128)} %bitcast.5, f32[288,128]{1,0:T(8,128)} %bitcast.4), custom_call_target="tpu_custom_call" | custom-call | tf_op jit(solution)/shard_map/pallas_call | solution.py:530
  78.9 1.5 %copy.5 = f32[2,24,1,512]{3,2,1,0:T(1,128)} copy(f32[2,24,1,512]{3,2,1,0:T(1,128)} %bitcast.3) | data formatting | bytes 196608

commit v3 on v2

--- a/solution.py
+++ b/solution.py
@@ -16,7 +16,9 @@
 gamma_block = (((1, 1), (0, 1)), ((1, 2), (0, 0)), ((0, 1), (1, 3)), ((0, 0), (1, 0)))
 gamma_adjoint = (((1, 3), (0, 3)), ((1, 0), (0, 2)), ((0, 3), (1, 1)), ((0, 0), (1, 0)))
 NX, NY, NHI, NC = 4, 4, 4, 2
-Z_OFFSET = 28
+Z_OFFSET = 7
+Z_SIGN = -1
+ROUNDS = 3
 TP, TM, KP, KM, SP, SM = range(6)
 
 
@@ -108,6 +110,7 @@
     send2,
     recv2,
     local,
+    phase,
 ):
     nz = NHI * nlo
     nt = nz * NC
@@ -120,7 +123,10 @@
     def device(dx, dy, dz, dc):
         return (dy * NHI + lax.div(dz, nlo), lax.rem(dz, nlo) * (NX * NC) + dx * NC + dc)
 
-    z_to = lax.rem(lax.div(p, NC) + Z_OFFSET, nz)
+    def z_of(time):
+        return lax.rem(Z_SIGN * lax.div(time, NC) + Z_OFFSET + nz, nz)
+
+    z_to = z_of(p)
     upper = f >= 8
     folded = jnp.where(upper, 15 - f, f)
     y_to = lax.rem(NY - lax.div(folded, 2), NY)
@@ -129,7 +135,7 @@
     ahead = lax.rem(z_to - zlo + nz, nz)
     gives_links = zhi == lax.rem(lax.div(ahead + nlo // 2, nlo), NHI)
     to_self = (y_to == y) & (z_to == z)
-    t = lax.rem(z + nz - Z_OFFSET % nz, nz) * NC + c
+    t = lax.rem(Z_SIGN * (z - Z_OFFSET) + nz + nz, nz) * NC + c
     seg = lax.rem(NY - y, NY)
     sources = (2 * seg, 2 * seg + 1, 15 - 2 * seg, 14 - 2 * seg)
     ahead_me = lax.rem(z - lax.div(t, NX * NC) + nz, nz)
@@ -137,8 +143,8 @@
 
     t_up, t_down = lax.rem(t + 1, nt), lax.rem(t + nt - 1, nt)
     near = {
-        TP: device(x, y, lax.rem(lax.div(t_up, NC) + Z_OFFSET, nz), lax.rem(t_up, NC)),
-        TM: device(x, y, lax.rem(lax.div(t_down, NC) + Z_OFFSET, nz), lax.rem(t_down, NC)),
+        TP: device(x, y, z_of(t_up), lax.rem(t_up, NC)),
+        TM: device(x, y, z_of(t_down), lax.rem(t_down, NC)),
         KP: device(lax.rem(x + 1, NX), y, z, c),
         KM: device(lax.rem(x + NX - 1, NX), y, z, c),
         SP: device(x, lax.rem(y + NY - 1, NY), z, c),
@@ -432,18 +438,23 @@
             device_id_type=MESH,
         )
 
-    for early in (True, False):
+    for hi in range(NHI):
         for n in range(4):
-            first = (lax.rem(sources[n], NHI) < 2) if early else (lax.rem(sources[n], NHI) >= 2)
-
-            @pl.when(jnp.logical_not(to_self & (slot == n)) & first)
+
+            @pl.when(jnp.logical_not(to_self & (slot == n)) & (lax.rem(sources[n], NHI) == hi))
             def _():
                 back_copy(n).start()
 
-        if early:
+        if hi == 0:
+            for r in range(ROUNDS):
+                for side in (KP, KM):
+                    pl.semaphore_signal(phase.at[r], inc=1, device_id=near[side], device_id_type=MESH)
+                pl.semaphore_wait(phase.at[r], 2)
+
+        if hi < NHI - 1:
             for n in range(4):
 
-                @pl.when(jnp.logical_not(to_self & (slot == n)) & (lax.rem(sources[n], NHI) < 2))
+                @pl.when(jnp.logical_not(to_self & (slot == n)) & (lax.rem(sources[n], NHI) == hi))
                 def _():
                     back_copy(n).wait_send()
 
@@ -512,7 +523,7 @@
 
     for n in range(4):
 
-        @pl.when(jnp.logical_not(to_self & (slot == n)) & (lax.rem(sources[n], NHI) >= 2))
+        @pl.when(jnp.logical_not(to_self & (slot == n)) & (lax.rem(sources[n], NHI) == NHI - 1))
         def _():
             back_copy(n).wait_send()
 
@@ -559,6 +570,7 @@
                 dma((4,)),
                 dma((4,)),
                 dma((4,)),
+                pltpu.SemaphoreType.REGULAR((ROUNDS,)),
             ],
             compiler_params=pltpu.CompilerParams(
                 collective_id=0, has_side_effects=True, vmem_limit_bytes=60 * 2**20

time: 80.6 us -> 76.9 us (0.954)
  the two profiles are of different devices: /device:TPU:160 before, /device:TPU:360 now
where the time goes in v3:
time: 76.9 us; the launch traced here: 76.7 us
  Pallas kernels  75.2 us (98%)
  local copies, waits for them, and re-layouts  1.54 us (2%)
    pallas_call x1, Pallas kernels, on_device(): pl.pallas_call(functools.partial(kernel, nlo), out_shape=jax.ShapeDtypeSt...  75.2 us
    unnamed x1, local copies, waits for them, and re-layouts  1.54 us

profile of v3, /device:TPU:360, one launch (start us, length us, event | category | flops | bytes accessed | tf_op | source)
XLA Modules:
  0.0 76.7 jit_solution(661617768176009779)
XLA Ops:
  0.0 75.2 %shard_map.28 = f32[192,128]{1,0:T(8,128)} custom-call(f32[192,128]{1,0:T(8,128)} %bitcast.5, f32[288,128]{1,0:T(8,128)} %bitcast.4), custom_call_target="tpu_custom_call" | custom-call | tf_op jit(solution)/shard_map/pallas_call | solution.py:541
  75.2 1.5 %copy.5 = f32[2,24,1,512]{3,2,1,0:T(1,128)} copy(f32[2,24,1,512]{3,2,1,0:T(1,128)} %bitcast.3) | data formatting | bytes 196608

commit v4 on v3

--- a/solution.py
+++ b/solution.py
@@ -18,7 +18,6 @@
 NX, NY, NHI, NC = 4, 4, 4, 2
 Z_OFFSET = 7
 Z_SIGN = -1
-ROUNDS = 3
 TP, TM, KP, KM, SP, SM = range(6)
 
 
@@ -110,7 +109,6 @@
     send2,
     recv2,
     local,
-    phase,
 ):
     nz = NHI * nlo
     nt = nz * NC
@@ -176,18 +174,12 @@
     for source, target, sem in ((sp_hbm, sp_ref, 2), (g_hbm, g_ref, 3)):
         pltpu.make_async_copy(source, target, local.at[sem]).start()
     pltpu.make_async_copy(sp_hbm, sp_ref, local.at[2]).wait()
-    pltpu.make_async_copy(g_hbm, g_ref, local.at[3]).wait()
 
     for q in range(NX):
         for s in range(2):
             for b in range(3):
                 row = pl.multiple_of(q * 48 + lax.rem(s + flip, 2) * 24 + b * 8, 8)
                 stage[pl.ds(row, 8), :] = sp_ref[pl.ds((s * 24 + b * 8) * 4 + q, 8, stride=4), :]
-        for mu in range(4):
-            first = g_ref[pl.ds(mu * 72 + q, 8, stride=4), :]
-            gstage[q * 48 + mu * 12 : q * 48 + mu * 12 + 8, :] = first
-            last = g_ref[pl.ds(mu * 72 + 32 + q, 4, stride=4), :]
-            gstage[q * 48 + mu * 12 + 8 : q * 48 + mu * 12 + 12, :] = last
 
     count = 8 - jnp.where(to_self, 1, 0) + jnp.where(seg > 0, 1, 0) + jnp.where(seg < NY - 1, 1, 0)
     pl.semaphore_wait(barrier, count)
@@ -223,7 +215,20 @@
         def _():
             out_copy(q).start()
 
-        @pl.when(other & gives_links)
+    pltpu.make_async_copy(g_hbm, g_ref, local.at[3]).wait()
+
+    @pl.when(gives_links)
+    def _():
+        for q in range(NX):
+            for mu in range(4):
+                first = g_ref[pl.ds(mu * 72 + q, 8, stride=4), :]
+                gstage[q * 48 + mu * 12 : q * 48 + mu * 12 + 8, :] = first
+                last = g_ref[pl.ds(mu * 72 + 32 + q, 4, stride=4), :]
+                gstage[q * 48 + mu * 12 + 8 : q * 48 + mu * 12 + 12, :] = last
+
+    for q in range(NX):
+
+        @pl.when(jnp.logical_not(to_self & (x == q)) & gives_links)
         def _():
             link_copy(q).start()
 
@@ -445,12 +450,6 @@
             def _():
                 back_copy(n).start()
 
-        if hi == 0:
-            for r in range(ROUNDS):
-                for side in (KP, KM):
-                    pl.semaphore_signal(phase.at[r], inc=1, device_id=near[side], device_id_type=MESH)
-                pl.semaphore_wait(phase.at[r], 2)
-
         if hi < NHI - 1:
             for n in range(4):
 
@@ -541,7 +540,7 @@
         out = pl.pallas_call(
             functools.partial(kernel, nlo),
             out_shape=jax.ShapeDtypeStruct((192, 128), jnp.float32),
-            in_specs=[pl.BlockSpec(memory_space=pl.ANY)] * 2,
+            in_specs=[pl.BlockSpec(memory_space=pltpu.HBM)] * 2,
             out_specs=vmem,
             scratch_shapes=[
                 f32(192, 128),
@@ -570,10 +569,9 @@
                 dma((4,)),
                 dma((4,)),
                 dma((4,)),
-                pltpu.SemaphoreType.REGULAR((ROUNDS,)),
             ],
             compiler_params=pltpu.CompilerParams(
-                collective_id=0, has_side_effects=True, vmem_limit_bytes=60 * 2**20
+                collective_id=0, has_side_effects=True, vmem_limit_bytes=55104 * 1024
             ),
         )(spinor.reshape(192, 128), gauge_links.reshape(288, 128))
         return out.reshape(2, 24, 1, 512)

time: 76.9 us -> 77.8 us (1.012)
  the two profiles are of different devices: /device:TPU:360 before, /device:TPU:142 now
where the time goes in v4:
time: 77.8 us; the launch traced here: 77.6 us
  Pallas kernels  77 us (99%)
    pallas_call x1, Pallas kernels, on_device(): pl.pallas_call(functools.partial(kernel, nlo), out_shape=jax.ShapeDtypeSt...  77 us

profile of v4, /device:TPU:142, one launch (start us, length us, event | category | flops | bytes accessed | tf_op | source)
XLA Modules:
  0.0 77.6 jit_solution(12549858433933366312)
XLA Ops:
  0.0 77.0 %shard_map.28 = f32[192,128]{1,0:T(8,128)S(1)} custom-call(f32[192,128]{1,0:T(8,128)} %bitcast.5, f32[288,128]{1,0:T(8,128)} %bitcast.4), custom_call_target="tpu_custom_call" | custom-call | tf_op jit(solution)/shard_map/pallas_call | solution.py:540
  77.0 0.6 copy.5

commit v5 on v3

--- a/solution.py
+++ b/solution.py
@@ -16,9 +16,8 @@
 gamma_block = (((1, 1), (0, 1)), ((1, 2), (0, 0)), ((0, 1), (1, 3)), ((0, 0), (1, 0)))
 gamma_adjoint = (((1, 3), (0, 3)), ((1, 0), (0, 2)), ((0, 3), (1, 1)), ((0, 0), (1, 0)))
 NX, NY, NHI, NC = 4, 4, 4, 2
-Z_OFFSET = 7
+Z_OFFSET = 5
 Z_SIGN = -1
-ROUNDS = 3
 TP, TM, KP, KM, SP, SM = range(6)
 
 
@@ -110,7 +109,6 @@
     send2,
     recv2,
     local,
-    phase,
 ):
     nz = NHI * nlo
     nt = nz * NC
@@ -445,12 +443,6 @@
             def _():
                 back_copy(n).start()
 
-        if hi == 0:
-            for r in range(ROUNDS):
-                for side in (KP, KM):
-                    pl.semaphore_signal(phase.at[r], inc=1, device_id=near[side], device_id_type=MESH)
-                pl.semaphore_wait(phase.at[r], 2)
-
         if hi < NHI - 1:
             for n in range(4):
 
@@ -541,7 +533,7 @@
         out = pl.pallas_call(
             functools.partial(kernel, nlo),
             out_shape=jax.ShapeDtypeStruct((192, 128), jnp.float32),
-            in_specs=[pl.BlockSpec(memory_space=pl.ANY)] * 2,
+            in_specs=[pl.BlockSpec(memory_space=pltpu.HBM)] * 2,
             out_specs=vmem,
             scratch_shapes=[
                 f32(192, 128),
@@ -570,10 +562,9 @@
                 dma((4,)),
                 dma((4,)),
                 dma((4,)),
-                pltpu.SemaphoreType.REGULAR((ROUNDS,)),
             ],
             compiler_params=pltpu.CompilerParams(
-                collective_id=0, has_side_effects=True, vmem_limit_bytes=60 * 2**20
+                collective_id=0, has_side_effects=True, vmem_limit_bytes=55104 * 1024
             ),
         )(spinor.reshape(192, 128), gauge_links.reshape(288, 128))
         return out.reshape(2, 24, 1, 512)

time: 76.9 us -> 73 us (0.949)
  the two profiles are of different devices: /device:TPU:360 before, /device:TPU:130 now
where the time goes in v5:
time: 73 us; the launch traced here: 72.8 us
  Pallas kernels  72.2 us (99%)
    pallas_call x1, Pallas kernels, on_device(): pl.pallas_call(functools.partial(kernel, nlo), out_shape=jax.ShapeDtypeSt...  72.2 us

profile of v5, /device:TPU:130, one launch (start us, length us, event | category | flops | bytes accessed | tf_op | source)
XLA Modules:
  0.0 72.8 jit_solution(15850498758653136489)
XLA Ops:
  0.0 72.2 %shard_map.28 = f32[192,128]{1,0:T(8,128)S(1)} custom-call(f32[192,128]{1,0:T(8,128)} %bitcast.5, f32[288,128]{1,0:T(8,128)} %bitcast.4), custom_call_target="tpu_custom_call" | custom-call | tf_op jit(solution)/shard_map/pallas_call | solution.py:533
  72.2 0.6 copy.5

commit v6 on v5

--- a/solution.py
+++ b/solution.py
@@ -217,13 +217,15 @@
     for q in range(NX):
         other = jnp.logical_not(to_self & (x == q))
 
-        @pl.when(other)
+        @pl.when(other & gives_links)
+        def _():
+            link_copy(q).start()
+
+    for q in range(NX):
+
+        @pl.when(jnp.logical_not(to_self & (x == q)))
         def _():
             out_copy(q).start()
-
-        @pl.when(other & gives_links)
-        def _():
-            link_copy(q).start()
 
     @pl.when(to_self)
     def _():

time: 73 us -> 72.9 us (level)
  no operation moved by 1% of the time
where the time goes in v6:
time: 72.9 us; the launch traced here: 72.8 us
  Pallas kernels  72.1 us (99%)
    pallas_call x1, Pallas kernels, on_device(): pl.pallas_call(functools.partial(kernel, nlo), out_shape=jax.ShapeDtypeSt...  72.1 us

profile of v6, /device:TPU:130, one launch (start us, length us, event | category | flops | bytes accessed | tf_op | source)
XLA Modules:
  0.0 72.8 jit_solution(12060618190233944649)
XLA Ops:
  0.0 72.1 %shard_map.28 = f32[192,128]{1,0:T(8,128)S(1)} custom-call(f32[192,128]{1,0:T(8,128)} %bitcast.5, f32[288,128]{1,0:T(8,128)} %bitcast.4), custom_call_target="tpu_custom_call" | custom-call | tf_op jit(solution)/shard_map/pallas_call | solution.py:535
  72.1 0.6 copy.5
